TPU v7x, 32 devices: a whole 2x2x4 slice. The times are simulated.
32 devices in a mesh: ctx: 2 (over core), exp: 16 (over z, y, x).
Axes of the slice: x: 2, y: 2, z: 4, core: 2. Of those that a mesh axis runs over, the one named last changes fastest.
Arguments:
- queries: bfloat16 [1024, 4096], P('ctx', 'exp'), may hold values from -32 to 32
- keys: bfloat16 [1024, 4096], P('ctx', 'exp'), may hold values from -4 to 4
- values: bfloat16 [1024, 4096], P('ctx', 'exp'), may hold values from -6 to 6
- out_proj: bfloat16 [4096, 3584], P('exp'), may hold values from -0.5 to 0.5
- residual: bfloat16 [1024, 3584], P(('ctx', 'exp')), may hold values from -6 to 6
- norm_gain: float32 [3584], replicated, may hold values from 0.25 to 1.75
- routes: int32 [1024, 8], P(('ctx', 'exp')), may hold values from 0 to 15, all different within a row; in each aligned block of 32 rows (0 to 31, 32 to 63, ...) at most 20 rows name the same one
- combine: float32 [1024, 8], P(('ctx', 'exp')), may hold values from 0.1 to 0.5
- w_gate: bfloat16 [16, 3584, 1024], P('exp', None, 'ctx'), may hold values from -0.09375 to 0.09375
- w_up: bfloat16 [16, 3584, 1024], P('exp', None, 'ctx'), may hold values from -0.09375 to 0.09375
- w_down: bfloat16 [16, 1024, 3584], P('exp', 'ctx'), may hold values from -0.1875 to 0.1875
Outputs:
- layer_out: bfloat16 [1024, 3584], P(('ctx', 'exp'))
Inputs may be any that keep to these rules, and one draw needn't show every extreme that they name: `routes`: each row names 8 different experts. Within each aligned block of 32 rows no expert is named by more than 20 rows, and some block names some expert exactly 20 times.
All inputs are finite; a program needn't handle non-finite values.
Results may differ from a plain program's by a relative error of at most 0.023.
Values may be sent and summed in bfloat16 or wider, within the bound.
A program may use at most 128 MiB of HBM per device.

v0:
```python
import math

import jax
import jax.numpy as jnp
from jax import lax
from jax.sharding import PartitionSpec as P

HD = 128


masked_score = -1e30
norm_eps = 1e-06


def from_behind(shard, axis, by):
    peers = lax.axis_size(axis)
    pairs = [(i, i + by) for i in range(peers) if 0 <= i + by < peers]
    return lax.ppermute(shard, axis, pairs)


def per_device(
    queries, keys, values, out_proj, residual, norm_gain, routes, combine, w_gate, w_up, w_down
):
    query_rows = queries.shape[0]
    head_count = queries.shape[1] // HD
    scaling = 1.0 / math.sqrt(HD)
    ctx_where = lax.axis_index("ctx")
    ctx_count = lax.axis_size("ctx")

    def attend(carried, query_heads, pair_block, visible):
        key_count = pair_block.shape[1]
        key_heads = pair_block[0].reshape(key_count, head_count, HD)
        value_heads = pair_block[1].reshape(key_count, head_count, HD)
        scores = (
            jnp.einsum("qhd,khd->hqk", query_heads, key_heads, preferred_element_type=jnp.float32)
            * scaling
        )
        scores = jnp.where(visible, scores, masked_score)
        peak_old, total_old, weighted_old = carried
        peak_new = jnp.maximum(peak_old, jnp.max(scores, axis=2))
        expo_block = jnp.exp(scores - peak_new[:, :, None])
        factor = jnp.exp(peak_old - peak_new)
        total_new = total_old * factor + jnp.sum(expo_block, axis=2)
        weighted_new = weighted_old * factor.T[:, :, None] + jnp.einsum(
            "hqk,khd->qhd",
            expo_block.astype(jnp.bfloat16),
            value_heads,
            preferred_element_type=jnp.float32,
        )
        return (peak_new, total_new, weighted_new)

    initial = (
        jnp.full((head_count, query_rows), masked_score, jnp.float32),
        jnp.zeros((head_count, query_rows), jnp.float32),
        jnp.zeros((query_rows, head_count, HD), jnp.float32),
    )
    query_heads = queries.reshape(query_rows, head_count, HD)
    row_ids = jnp.arange(query_rows)
    diag_mask = row_ids[:, None] >= row_ids[None, :]
    pair_block = jnp.stack([keys, values])
    carried = attend(initial, query_heads, pair_block, diag_mask)
    for step_index in range(1, ctx_count):
        pair_block = from_behind(pair_block, "ctx", 1)
        carried = attend(carried, query_heads, pair_block, ctx_where >= step_index)
    attended = (
        (carried[2] / carried[1].T[:, :, None])
        .astype(jnp.bfloat16)
        .reshape(query_rows, head_count * HD)
    )
    tok_count = residual.shape[0]
    term = jnp.dot(attended, out_proj, preferred_element_type=jnp.float32)
    mixed = lax.psum_scatter(
        lax.optimization_barrier(term.astype(jnp.bfloat16))
        .astype(jnp.float32)
        .astype(jnp.bfloat16),
        "exp",
        scatter_dimension=0,
        tiled=True,
    ).astype(jnp.float32)
    stream = residual.astype(jnp.float32) + mixed
    normed = (
        stream * lax.rsqrt(jnp.mean(stream * stream, axis=1, keepdims=True) + norm_eps) * norm_gain
    ).astype(jnp.bfloat16)
    width = normed.shape[1]
    per_token = routes.shape[1]
    experts = lax.axis_size("exp")
    capacity = min(tok_count, max(2, tok_count * per_token * 5 // (4 * experts)))
    pair_count = tok_count * per_token
    flat_routes = routes.reshape(pair_count)
    expert_hot = (flat_routes[:, None] == jnp.arange(experts)[None, :]).astype(jnp.int32)
    earlier = jnp.cumsum(expert_hot, axis=0) - expert_hot
    slot_index = jnp.sum(earlier * expert_hot, axis=1)
    position = flat_routes * capacity + slot_index
    position_hot = (position[:, None] == jnp.arange(experts * capacity)[None, :]).astype(
        jnp.float32
    )
    token_hot = (
        (jnp.arange(pair_count) // per_token)[:, None] == jnp.arange(tok_count)[None, :]
    ).astype(jnp.float32)
    pick_rows = jnp.einsum("pr,pt->rt", position_hot, token_hot).astype(jnp.bfloat16)
    outgoing = (
        jnp.dot(pick_rows, normed, preferred_element_type=jnp.float32)
        .astype(jnp.bfloat16)
        .reshape(experts, capacity, width)
    )
    received = lax.all_to_all(outgoing, "exp", split_axis=0, concat_axis=0, tiled=True)
    gate_local = w_gate[0]
    up_local = w_up[0]
    down_local = w_down[0]
    piece = lax.all_gather(received, "ctx", axis=0, tiled=True)
    gate = jnp.einsum("smd,df->smf", piece, gate_local, preferred_element_type=jnp.float32)
    upper = jnp.einsum("smd,df->smf", piece, up_local, preferred_element_type=jnp.float32)
    act_all = (jax.nn.silu(gate) * upper).astype(jnp.bfloat16)
    expert_out = lax.psum_scatter(
        jnp.einsum("smf,fd->smd", act_all, down_local, preferred_element_type=jnp.float32).astype(
            jnp.bfloat16
        ),
        "ctx",
        scatter_dimension=0,
        tiled=True,
    )
    returned = lax.all_to_all(expert_out, "exp", split_axis=0, concat_axis=0, tiled=True)
    weigh_rows = jnp.einsum(
        "pr,pt->tr", position_hot, token_hot * combine.reshape(pair_count)[:, None]
    )
    moe_sum = jnp.dot(
        weigh_rows,
        returned.reshape(experts * capacity, width).astype(jnp.float32),
        precision=lax.Precision.HIGHEST,
    )
    return (stream + moe_sum).astype(jnp.bfloat16)


def solution(mesh):
    in_specs = (
        P("ctx", "exp"),
        P("ctx", "exp"),
        P("ctx", "exp"),
        P("exp", None),
        P(("ctx", "exp"), None),
        P(),
        P(("ctx", "exp"), None),
        P(("ctx", "exp"), None),
        P("exp", None, "ctx"),
        P("exp", None, "ctx"),
        P("exp", "ctx", None),
    )
    out_specs = P(("ctx", "exp"), None)
    return jax.shard_map(
        per_device, mesh=mesh, in_specs=in_specs, out_specs=out_specs, check_vma=False
    )
```

profile of v0, /device:TPU:14, one launch (start us, length us, event | category | flops | bytes accessed | tf_op | source)
XLA Modules:
  0.0 316.5 jit_solution(6986413845431565366)
XLA Ops:
  6.5 0.0 copy-start
  6.5 0.0 copy-start.3
  6.5 0.0 reduce-scatter.3.cloned.1.call-start
  6.5 1.2 copy.53
  7.8 1.1 copy.39
  8.9 0.1 pad_maximum_fusion
  8.9 1.8 collective-permute-start
  10.7 0.1 iota_compare_fusion
  10.8 0.0 copy-done.3
  10.8 1.5 fusion.7
  12.3 0.0 collective-permute-done
  12.4 0.5 bitcast_reduce_fusion
  12.9 0.6 fusion.10
  13.5 0.5 fusion.8
  14.0 0.7 fusion.19
  14.8 0.7 fusion.22
  15.5 0.0 copy-done
  15.5 3.0 convolution_convert_fusion.1
  18.5 0.0 copy-start.5
  18.5 0.0 copy-start.1
  18.5 0.0 copy-start.4
  18.5 0.0 reduce-scatter.3.cloned.1.call-update
  18.5 0.0 all-gather.2.cloned.1.call-start
  18.6 0.6 copy-done.5
  19.2 0.1 copy.45
  19.2 0.1 eq.61
  19.3 0.1 reshape.76
  19.4 0.6 reduce-window.6
  20.0 0.2 slice_reduce_fusion
  20.2 0.1 fusion.57
  20.3 82.6 %reduce-scatter.3.cloned.1.call-done = bf16[32,3584]{1,0:T(8,128)(2,1)} async-done(((bf16[512,3584]{1,0:T(8,128)(2,1)}), bf16[32,3584]{1,0:T(8,128)(2,1)}) %reduce-scatter.3.cloned.1.call-update) | async-done | bytes 229392 | tf_op jit(solution)/shard_map/reduce_scatter | solution.py:72
  102.9 0.0 copy-done.1
  102.9 1.1 multiply_reduce_fusion
  104.0 0.0 copy-done.4
  104.0 3.4 %convolution_convert_fusion.2 = bf16[320,3584]{1,0:T(8,128)(2,1)} fusion(bf16[32,3584]{1,0:T(8,128)(2,1)} %reduce-scatter.3.cloned.1.call-done, bf16[32,3584]{1,0:T(8,128)(2,1)S(1)} %copy-done.1, f32[3584]{0:T(1024)S(1)} %copy-done.4, f32[32]{0:T(128)S(1)} %add_rsqrt_fusion, s32[256]{0:T(256)S(1)} %get-tuple-element.17, s32[256]{0:T(256)S(1)} %get-tuple-element.16), kind=kOutput, calls=%fused_computation.2 | convolution fusion | flops 80578560 | bytes 2769024 | tf_op jit(solution)/shard_map/dot_general | solution.py:102
  107.4 4.1 %reshape.78 = bf16[16,20,3584]{2,1,0:T(8,128)(2,1)} reshape(bf16[320,3584]{1,0:T(8,128)(2,1)} %convolution_convert_fusion.2) | data formatting | bytes 4587520 | tf_op jit(solution)/shard_map/reshape | solution.py:104
  111.5 67.6 %all_to_all.10 = bf16[16,20,3584]{2,1,0:T(8,128)(2,1)S(1)} all-to-all(bf16[16,20,3584]{2,1,0:T(8,128)(2,1)} %reshape.78), channel_id=1, replica_groups=mesh['ctx'=2,'exp'=16] {'exp'}, dimensions={0} | all-to-all | bytes 4587520 | tf_op jit(solution)/shard_map/all_to_all | solution.py:106
  179.1 2.1 copy.48
  181.2 0.0 all-gather.2.cloned.1.call-update
  181.3 0.2 reduce-scatter.5.cloned.1.call-start
  181.5 14.6 %all-gather.2.cloned.1.call-done = bf16[32,20,3584]{2,0,1:T(8,128)(2,1)} async-done(((bf16[16,20,3584]{2,0,1:T(8,128)(2,1)}), bf16[32,20,3584]{2,0,1:T(8,128)(2,1)}) %all-gather.2.cloned.1.call-update) | async-done | bytes 4587536 | tf_op jit(solution)/shard_map/all_gather | solution.py:110
  196.1 6.0 %fusion.4 = f32[32,20,512]{2,0,1:T(8,128)S(1)} fusion(bf16[32,20,3584]{2,0,1:T(8,128)(2,1)} %all-gather.2.cloned.1.call-done, bf16[1,3584,512]{2,1,0:T(8,128)(2,1)} %param.19), kind=kOutput, calls=%fused_computation.8 | convolution fusion | flops 2348810240 | bytes 9568256 | tf_op jit(solution)/shard_map/smd,df->smf/dot_general | solution.py:111
  202.1 11.6 %convolution_convert_fusion = bf16[32,20,3584]{2,0,1:T(8,128)(2,1)} fusion(bf16[1,512,3584]{2,1,0:T(8,128)(2,1)} %param.21, bf16[32,20,3584]{2,0,1:T(8,128)(2,1)} %all-gather.2.cloned.1.call-done, bf16[1,3584,512]{2,1,0:T(8,128)(2,1)} %param.20, f32[32,20,512]{2,0,1:T(8,128)S(1)} %fusion.4), kind=kOutput, calls=%fused_computation | convolution fusion | flops 4701880320 | bytes 17825792 | tf_op jit(solution)/shard_map/smf,fd->smd/dot_general | solution.py:115
  213.6 0.0 reduce-scatter.5.cloned.1.call-update
  213.7 13.8 %reduce-scatter.5.cloned.1.call-done = bf16[16,20,3584]{2,0,1:T(8,128)(2,1)} async-done(((bf16[32,20,3584]{2,0,1:T(8,128)(2,1)}), bf16[16,20,3584]{2,0,1:T(8,128)(2,1)}) %reduce-scatter.5.cloned.1.call-update) | async-done | bytes 2293776 | tf_op jit(solution)/shard_map/reduce_scatter | solution.py:114
  227.5 4.5 %copy.49 = bf16[16,20,3584]{2,1,0:T(8,128)(2,1)} copy(bf16[16,20,3584]{2,0,1:T(8,128)(2,1)} %reduce-scatter.5.cloned.1.call-done) | data formatting | bytes 4587520 | tf_op jit(solution)/shard_map/reduce_scatter | solution.py:114
  231.9 0.0 copy-start.6
  231.9 7.1 %all-to-all-start.1 = ((bf16[16,20,3584]{2,1,0:T(8,128)(2,1)}), bf16[16,20,3584]{2,1,0:T(8,128)(2,1)}, u32[]{:S(2)}, u32[]{:S(2)}) async-start(bf16[16,20,3584]{2,1,0:T(8,128)(2,1)} %copy.49), calls=%async_computation.3 | async-start | bytes 5505024 | tf_op jit(solution)/shard_map/all_to_all | solution.py:122
  239.0 0.0 copy-done.6
  239.0 0.1 copy.44
  239.1 0.1 mul.79
  239.2 0.3 fusion.35
  239.5 0.0 copy-start.2
  239.5 62.7 %all-to-all-done.1 = bf16[16,20,3584]{2,1,0:T(8,128)(2,1)} async-done(((bf16[16,20,3584]{2,1,0:T(8,128)(2,1)}), bf16[16,20,3584]{2,1,0:T(8,128)(2,1)}, u32[]{:S(2)}, u32[]{:S(2)}) %all-to-all-start.1) | async-done | bytes 2293792 | tf_op jit(solution)/shard_map/all_to_all | solution.py:122
  302.3 4.1 %reshape.79 = bf16[320,3584]{1,0:T(8,128)(2,1)} reshape(bf16[16,20,3584]{2,1,0:T(8,128)(2,1)} %all-to-all-done.1) | data formatting | bytes 4587520 | tf_op jit(solution)/shard_map/reshape | solution.py:128
  306.4 0.0 copy-done.2
  306.4 3.6 %fusion = bf16[32,3584]{1,0:T(8,128)(2,1)} fusion(f32[32,320]{1,0:T(8,128)S(1)} %fusion.35, bf16[320,3584]{1,0:T(8,128)(2,1)} %reshape.79, bf16[32,3584]{1,0:T(8,128)(2,1)S(1)} %copy-done.2, bf16[32,3584]{1,0:T(8,128)(2,1)S(1)} %copy-done.1), kind=kOutput, calls=%fused_computation.4 | convolution fusion | flops 440975360 | bytes 3022848 | tf_op jit(solution)/shard_map/dot_general | solution.py:126
  (8 shorter events, 0.1 us)
Async XLA Ops:
  6.5 9.0 %copy-start = (bf16[256,3584]{1,0:T(8,128)(2,1)S(1)}, bf16[256,3584]{1,0:T(8,128)(2,1)}, u32[]{:S(2)}) copy-start(bf16[256,3584]{1,0:T(8,128)(2,1)} %param.14) | copy-start | bytes 5505028
  6.5 4.3 %copy-start.3 = (bf16[512,256]{1,0:T(8,128)(2,1)S(1)}, bf16[512,256]{1,0:T(8,128)(2,1)}, u32[]{:S(2)}) copy-start(bf16[512,256]{1,0:T(8,128)(2,1)} %param.11) | copy-start | bytes 786436
  6.5 96.4 %reduce-scatter.3.cloned.1.call-start = ((), (), s32[]{:S(2)}) async-start(), calls=%async_computation.4 | async-start | bytes 3899392 | tf_op jit(solution)/shard_map/reduce_scatter | solution.py:72
  8.9 3.4 %collective-permute-start = (bf16[2,512,256]{1,2,0:T(8,128)(2,1)S(1)}, bf16[2,512,256]{1,2,0:T(8,128)(2,1)S(1)}, u32[]{:S(2)}, u32[]{:S(2)}) collective-permute-start(bf16[2,512,256]{1,2,0:T(8,128)(2,1)S(1)} %pad_maximum_fusion), channel_id=1, source_target_pairs={{0,16},{1,17},{2,18},{3,19},{4,20},{5,21},{6,22},{7,23},{8,24},{9,... | collective-permute-start | bytes 1572872 | tf_op jit(solution)/shard_map/ppermute | solution.py:18
  18.5 0.7 copy-start.5
  18.5 84.4 %copy-start.1 = (bf16[32,3584]{1,0:T(8,128)(2,1)S(1)}, bf16[32,3584]{1,0:T(8,128)(2,1)}, u32[]{:S(2)}) copy-start(bf16[32,3584]{1,0:T(8,128)(2,1)} %param.15) | copy-start | bytes 688132
  18.5 85.6 %copy-start.4 = (f32[3584]{0:T(1024)S(1)}, f32[3584]{0:T(1024)}, u32[]{:S(2)}) copy-start(f32[3584]{0:T(1024)} %param.16) | copy-start | bytes 43012
  18.5 177.6 %all-gather.2.cloned.1.call-start = ((), (), s32[]{:S(2)}) async-start(), calls=%async_computation.5 | async-start | bytes 6881280 | tf_op jit(solution)/shard_map/all_gather | solution.py:110
  181.3 46.2 %reduce-scatter.5.cloned.1.call-start = ((), (), s32[]{:S(2)}) async-start(), calls=%async_computation.6 | async-start | bytes 6881280 | tf_op jit(solution)/shard_map/reduce_scatter | solution.py:114
  231.9 7.1 %copy-start.6 = (f32[32,8]{0,1:T(8,128)S(1)}, f32[32,8]{0,1:T(8,128)}, u32[]{:S(2)}) copy-start(f32[32,8]{0,1:T(8,128)} %param.18) | copy-start | bytes 3076
  231.9 70.3 %all-to-all-start.1 = ((bf16[16,20,3584]{2,1,0:T(8,128)(2,1)}), bf16[16,20,3584]{2,1,0:T(8,128)(2,1)}, u32[]{:S(2)}, u32[]{:S(2)}) async-start(bf16[16,20,3584]{2,1,0:T(8,128)(2,1)} %copy.49), calls=%async_computation.3 | async-start | bytes 5505024 | tf_op jit(solution)/shard_map/all_to_all | solution.py:122
  239.5 66.9 %copy-start.2 = (bf16[32,3584]{1,0:T(8,128)(2,1)S(1)}, bf16[32,3584]{1,0:T(8,128)(2,1)}, u32[]{:S(2)}) copy-start(bf16[32,3584]{1,0:T(8,128)(2,1)} %reduce-scatter.3.cloned.1.call-done) | copy-start | bytes 688132
Sparse Core Ops, SparseCore 0:
  18.6 84.2 reduce-scatter.2
  181.4 14.6 all-gather.1
  213.8 13.6 reduce-scatter.4
where the time goes:
time: 317 us
  waiting for transfers between devices  174 us (55%)
  blocking collectives  67.6 us (21%)
  matrix products  31.2 us (10%)
  local copies, waits for them, and re-layouts  18.4 us (6%)
  between operations  13.3 us (4%)
  starting transfers between devices  9.13 us (3%)
    reduce_scatter x1, waiting for transfers between devices, per_device(): lax.psum_scatter(lax.optimization_barrier(term.astype(jnp.bfloat16)).asty...  82.6 us
    all_to_all x1, blocking collectives, per_device(): lax.all_to_all(outgoing, 'exp', split_axis=0, concat_axis=0, tiled=True)  67.6 us
    all_to_all x1, waiting for transfers between devices, per_device(): lax.all_to_all(expert_out, 'exp', split_axis=0, concat_axis=0, tiled=True)  62.7 us
    all_gather x1, waiting for transfers between devices, per_device(): piece = lax.all_gather(received, 'ctx', axis=0, tiled=True)  14.6 us
    reduce_scatter x1, waiting for transfers between devices, per_device(): lax.psum_scatter(jnp.einsum('smf,fd->smd', act_all, down_local, preferred...  13.8 us
    dot_general x1, matrix products, per_device(): jnp.einsum('smf,fd->smd', act_all, down_local, preferred_element_type=jnp...  11.6 us
    all_to_all x1, starting transfers between devices, per_device(): lax.all_to_all(expert_out, 'exp', split_axis=0, concat_axis=0, tiled=True)  7.09 us
  transfers between devices with their start and end apart: 5, of which 4 were waited for; matrix products, arithmetic and copies ran while one was open for 1% of the time, Pallas kernels for 0%

commit v1 on v0

--- a/solution.py
+++ b/solution.py
@@ -1,15 +1,419 @@
+import functools
 import math
 
 import jax
 import jax.numpy as jnp
 from jax import lax
+from jax.experimental import pallas as pl
+from jax.experimental.pallas import tpu as pltpu
 from jax.sharding import PartitionSpec as P
 
 HD = 128
+LANES = 128
+CHUNKS = 4
+VMEM_BUDGET = 58 * 1024 * 1024
 
 
 masked_score = -1e30
 norm_eps = 1e-06
+
+
+def exp_grid(experts):
+    fast = 2 if experts % 2 == 0 else 1
+    slow = 4 if (experts // fast) % 4 == 0 else 1
+    return slow, experts // (fast * slow), fast
+
+
+def layer_kernel(
+    sizes,
+    attended_ref,
+    proj_ref,
+    residual_ref,
+    gain_ref,
+    weigh_ref,
+    gate_hbm,
+    up_hbm,
+    down_hbm,
+    out_ref,
+    term,
+    mix_one,
+    mix_two,
+    mix_last,
+    stream,
+    tokens,
+    weights,
+    gate_w,
+    up_w,
+    down_w,
+    gate,
+    upper,
+    act,
+    parts,
+    sum_ctx,
+    sum_one,
+    sum_two,
+    sum_last,
+    mix_send,
+    mix_recv,
+    tok_send,
+    tok_recv,
+    sum_send,
+    sum_recv,
+    load_sem,
+):
+    rows, width = residual_ref.shape
+    chunks = term.shape[0]
+    cols = width // chunks
+    where_exp = lax.axis_index("exp")
+    block = sizes["y"] * sizes["x"]
+    coords = {
+        "c": lax.axis_index("ctx"),
+        "z": lax.div(where_exp, block),
+        "y": lax.rem(lax.div(where_exp, sizes["x"]), sizes["y"]),
+        "x": lax.rem(where_exp, sizes["x"]),
+    }
+
+    def peer(axis, ahead):
+        there = dict(coords)
+        there[axis] = lax.rem(coords[axis] + ahead, sizes[axis])
+        number = (there["z"] * sizes["y"] + there["y"]) * sizes["x"] + there["x"]
+        return (there["c"], number), there[axis]
+
+    loads = [
+        pltpu.make_async_copy(source, target, load_sem.at[i])
+        for i, (source, target) in enumerate(
+            ((gate_hbm, gate_w), (up_hbm, up_w), (down_hbm, down_w))
+        )
+    ]
+    for load in loads:
+        load.start()
+
+    barrier = pltpu.get_barrier_semaphore()
+    greeted = 0
+    for axis in ("c", "z", "y", "x"):
+        for ahead in range(1, sizes[axis]):
+            device, _ = peer(axis, ahead)
+            pl.semaphore_signal(
+                barrier, inc=1, device_id=device, device_id_type=pl.DeviceIdType.MESH
+            )
+            greeted += 1
+    pl.semaphore_wait(barrier, greeted)
+
+    pending = []
+
+    def remote(source, target, send_sem, recv_sem, device):
+        copy = pltpu.make_async_remote_copy(
+            src_ref=source,
+            dst_ref=target,
+            send_sem=send_sem,
+            recv_sem=recv_sem,
+            device_id=device,
+            device_id_type=pl.DeviceIdType.MESH,
+        )
+        copy.start()
+        pending.append(copy)
+        return copy
+
+    def order(chunk):
+        return ("x", "y") if chunk % 2 == 0 else ("y", "x")
+
+    def place(axes, fixed):
+        return tuple(fixed.get(axis, slice(None)) for axis in axes)
+
+    def scatter_start(buffer, axes, chunk, stage, done, axis, landing, sends, recvs):
+        copies = []
+        others = [a for a in axes if a not in done and a != axis]
+        for ahead in range(1, sizes[axis]):
+            device, value = peer(axis, ahead)
+            fixed = {a: coords[a] for a in done}
+            fixed[axis] = value
+            window = tuple(pl.ds(0, sizes[a]) for a in others)
+            copies.append(
+                remote(
+                    buffer.at[(chunk,) + place(axes, fixed)],
+                    landing.at[(chunk, ahead - 1) + window],
+                    sends.at[chunk, stage, ahead - 1],
+                    recvs.at[chunk, stage, ahead - 1],
+                    device,
+                )
+            )
+        return copies
+
+    def block_ids(axes):
+        ids = [()]
+        for axis in axes:
+            ids = [i + (j,) for i in ids for j in range(sizes[axis])]
+        return ids
+
+    def scatter_end(buffer, axes, chunk, done, axis, landing, copies):
+        for copy in copies:
+            copy.wait_recv()
+        others = [a for a in axes if a not in done and a != axis]
+        for ids in block_ids(others):
+            fixed = {a: coords[a] for a in done}
+            fixed[axis] = coords[axis]
+            fixed.update(zip(others, ids))
+            at = (chunk,) + place(axes, fixed)
+            total = buffer[at].astype(jnp.float32)
+            for slot in range(sizes[axis] - 1):
+                total = total + landing[(chunk, slot) + ids].astype(jnp.float32)
+            if others:
+                buffer[at] = total.astype(buffer.dtype)
+        return total
+
+    def gather_start(buffer, slot, stage, done, axis):
+        fixed = {a: coords[a] for a in ("c", "z", "y", "x") if a not in done}
+        copies = []
+        prefix = () if slot == chunks else (slot,)
+        view = buffer.at[prefix + place(("c", "z", "y", "x"), fixed)]
+        for ahead in range(1, sizes[axis]):
+            device, _ = peer(axis, ahead)
+            copies.append(
+                remote(
+                    view,
+                    view,
+                    tok_send.at[slot, stage, ahead - 1],
+                    tok_recv.at[slot, stage, ahead - 1],
+                    device,
+                )
+            )
+        return copies
+
+    flying = {}
+    here = (coords["c"], coords["z"], coords["y"], coords["x"])
+    weights[here] = weigh_ref[...]
+    weigh_axes = ("z", "y", "x", "c")
+
+    def weigh_step(stage):
+        if stage > 0:
+            for copy in flying["w", stage - 1]:
+                copy.wait_recv()
+        if stage < 4:
+            flying["w", stage] = gather_start(
+                weights, chunks, stage, weigh_axes[:stage], weigh_axes[stage]
+            )
+
+    grid_axes = ("z", "y", "x")
+    mix_landing = (mix_one, mix_two, mix_last)
+
+    def mix_axis(chunk, stage):
+        return (order(chunk) + ("z",))[stage]
+
+    def mix_start(chunk, stage):
+        done = (order(chunk) + ("z",))[:stage]
+        flying["m", chunk, stage] = scatter_start(
+            term, grid_axes, chunk, stage, done, mix_axis(chunk, stage),
+            mix_landing[stage], mix_send, mix_recv,
+        )
+
+    def mix_end(chunk, stage):
+        done = (order(chunk) + ("z",))[:stage]
+        return scatter_end(
+            term, grid_axes, chunk, done, mix_axis(chunk, stage),
+            mix_landing[stage], flying["m", chunk, stage],
+        )
+
+    attended = attended_ref[...]
+    squares = jnp.zeros((rows, 1), jnp.float32)
+    for step in range(chunks + 3):
+        if step < chunks:
+            span = pl.ds(step * cols, cols)
+            term[step] = (
+                jnp.dot(attended, proj_ref[:, span], preferred_element_type=jnp.float32)
+                .astype(jnp.bfloat16)
+                .reshape(term.shape[1:])
+            )
+            mix_start(step, 0)
+        for stage in (1, 2):
+            chunk = step - stage
+            if 0 <= chunk < chunks:
+                mix_end(chunk, stage - 1)
+                mix_start(chunk, stage)
+        chunk = step - 3
+        if 0 <= chunk < chunks:
+            span = pl.ds(chunk * cols, cols)
+            value = residual_ref[:, span].astype(jnp.float32) + mix_end(chunk, 2)
+            stream[:, span] = value
+            squares = squares + jnp.sum(value * value, axis=1, keepdims=True)
+        if step < 4:
+            weigh_step(step)
+    inverse = lax.rsqrt(squares / width + norm_eps)
+
+    def gather_axes(chunk):
+        first, second = order(chunk)
+        return ("z", second, first, "c")
+
+    def token_start(chunk, stage):
+        axes = gather_axes(chunk)
+        flying["t", chunk, stage] = gather_start(tokens, chunk, stage, axes[:stage], axes[stage])
+
+    for chunk in range(chunks):
+        span = pl.ds(chunk * cols, cols)
+        tokens[(chunk,) + here] = (stream[:, span] * inverse * gain_ref[:, span]).astype(
+            jnp.bfloat16
+        )
+        token_start(chunk, 0)
+    loads[0].wait()
+    loads[1].wait()
+    group_rows = gate.shape[1]
+    for step in range(1, chunks + 4):
+        for stage in (1, 2, 3):
+            chunk = step - stage
+            if 0 <= chunk < chunks:
+                for copy in flying["t", chunk, stage - 1]:
+                    copy.wait_recv()
+                token_start(chunk, stage)
+        chunk = step - 4
+        if 0 <= chunk < chunks:
+            for copy in flying["t", chunk, 3]:
+                copy.wait_recv()
+            span = pl.ds(chunk * cols, cols)
+
+            def grow(group, carry, chunk=chunk, span=span):
+                piece = tokens[chunk, group].reshape(group_rows, cols)
+                more_gate = jnp.dot(piece, gate_w[span, :], preferred_element_type=jnp.float32)
+                more_upper = jnp.dot(piece, up_w[span, :], preferred_element_type=jnp.float32)
+                if chunk > 0:
+                    more_gate = gate[group] + more_gate
+                    more_upper = upper[group] + more_upper
+                if chunk < chunks - 1:
+                    gate[group] = more_gate
+                    upper[group] = more_upper
+                else:
+                    act[group] = (jax.nn.silu(more_gate) * more_upper).astype(jnp.bfloat16)
+                return carry
+
+            lax.fori_loop(0, sizes["c"], grow, 0)
+
+    weigh_step(4)
+    loads[2].wait()
+
+    all_axes = ("c", "z", "y", "x")
+    sum_landing = (sum_ctx, sum_one, sum_two, sum_last)
+
+    def sum_axes(chunk):
+        return ("c",) + order(chunk) + ("z",)
+
+    def sum_start(chunk, stage):
+        axes = sum_axes(chunk)
+        flying["s", chunk, stage] = scatter_start(
+            parts, all_axes, chunk, stage, axes[:stage], axes[stage],
+            sum_landing[stage], sum_send, sum_recv,
+        )
+
+    def sum_end(chunk, stage):
+        axes = sum_axes(chunk)
+        return scatter_end(
+            parts, all_axes, chunk, axes[:stage], axes[stage],
+            sum_landing[stage], flying["s", chunk, stage],
+        )
+
+    lane = lax.broadcasted_iota(jnp.int32, (group_rows, LANES), 1)
+    for step in range(chunks + 4):
+        if step < chunks:
+            span = pl.ds(step * cols, cols)
+
+            def project(ahead, carry, step=step, span=span):
+                group = lax.rem(coords["c"] + ahead, sizes["c"])
+                held = weights[group].reshape(group_rows, LANES)
+                scale = jnp.sum(jnp.where(lane == where_exp, held, 0.0), axis=1, keepdims=True)
+                value = jnp.dot(act[group], down_w[:, span], preferred_element_type=jnp.float32)
+                parts[step, group] = (
+                    (value * scale).astype(jnp.bfloat16).reshape(parts.shape[2:])
+                )
+                return carry
+
+            lax.fori_loop(0, sizes["c"], project, 0)
+            sum_start(step, 0)
+        for stage in (1, 2, 3):
+            chunk = step - stage
+            if 0 <= chunk < chunks:
+                sum_end(chunk, stage - 1)
+                sum_start(chunk, stage)
+        chunk = step - 4
+        if 0 <= chunk < chunks:
+            span = pl.ds(chunk * cols, cols)
+            out_ref[:, span] = (stream[:, span] + sum_end(chunk, 3)).astype(jnp.bfloat16)
+    for copy in pending:
+        copy.wait_send()
+
+
+def layer_scratch(sizes, rows, width, hidden):
+    contexts, slow, mid, fast = (sizes[axis] for axis in ("c", "z", "y", "x"))
+    cols = width // CHUNKS
+    wide = max(mid, fast)
+    most = max(contexts, slow, wide) - 1
+    group = slow * mid * fast * rows
+    half, full = jnp.bfloat16, jnp.float32
+    one = (CHUNKS, wide - 1, slow, wide, rows, cols)
+    two = (CHUNKS, wide - 1, slow, rows, cols)
+    last = (CHUNKS, slow - 1, rows, cols)
+    grid = (slow, mid, fast, rows)
+    buffers = [
+        ((CHUNKS,) + grid + (cols,), half),
+        (one, half),
+        (two, half),
+        (last, half),
+        ((rows, width), full),
+        ((CHUNKS, contexts) + grid + (cols,), half),
+        ((contexts,) + grid + (LANES,), full),
+        ((width, hidden), half),
+        ((width, hidden), half),
+        ((hidden, width), half),
+        ((contexts, group, hidden), full),
+        ((contexts, group, hidden), full),
+        ((contexts, group, hidden), half),
+        ((CHUNKS, contexts) + grid + (cols,), half),
+        ((CHUNKS, contexts - 1) + grid + (cols,), half),
+        (one, half),
+        (two, half),
+        (last, half),
+    ]
+    size = sum(math.prod(shape) * (2 if kind == half else 4) for shape, kind in buffers)
+    semaphores = [
+        pltpu.SemaphoreType.DMA((CHUNKS, 3, most)),
+        pltpu.SemaphoreType.DMA((CHUNKS, 3, most)),
+        pltpu.SemaphoreType.DMA((CHUNKS + 1, 4, most)),
+        pltpu.SemaphoreType.DMA((CHUNKS + 1, 4, most)),
+        pltpu.SemaphoreType.DMA((CHUNKS, 4, most)),
+        pltpu.SemaphoreType.DMA((CHUNKS, 4, most)),
+        pltpu.SemaphoreType.DMA((3,)),
+    ]
+    return [pltpu.VMEM(shape, kind) for shape, kind in buffers] + semaphores, size
+
+
+def layer_sizes():
+    slow, mid, fast = exp_grid(lax.axis_size("exp"))
+    return {"c": lax.axis_size("ctx"), "z": slow, "y": mid, "x": fast}
+
+
+def fused_layer(attended, out_proj, residual, norm_gain, routes, combine, w_gate, w_up, w_down):
+    sizes = layer_sizes()
+    rows, width = residual.shape
+    scratch, _ = layer_scratch(sizes, rows, width, w_gate.shape[2])
+    named = routes[:, :, None] == jnp.arange(LANES)[None, None, :]
+    weigh = jnp.sum(jnp.where(named, combine[:, :, None], 0.0), axis=1)
+    in_vmem = pl.BlockSpec(memory_space=pltpu.VMEM)
+    anywhere = pl.BlockSpec(memory_space=pl.ANY)
+    return pl.pallas_call(
+        functools.partial(layer_kernel, sizes),
+        out_shape=jax.ShapeDtypeStruct((rows, width), jnp.bfloat16),
+        in_specs=[in_vmem] * 5 + [anywhere] * 3,
+        out_specs=in_vmem,
+        scratch_shapes=scratch,
+        compiler_params=pltpu.CompilerParams(
+            collective_id=0, has_side_effects=True, vmem_limit_bytes=VMEM_BUDGET
+        ),
+    )(
+        attended,
+        out_proj,
+        residual,
+        norm_gain.reshape(1, width),
+        weigh,
+        w_gate[0],
+        w_up[0],
+        w_down[0],
+    )
 
 
 def from_behind(shard, axis, by):
@@ -68,6 +472,13 @@
         .reshape(query_rows, head_count * HD)
     )
     tok_count = residual.shape[0]
+    _, scratch_bytes = layer_scratch(
+        layer_sizes(), tok_count, residual.shape[1], w_gate.shape[2]
+    )
+    if scratch_bytes < VMEM_BUDGET - 8 * 1024 * 1024 and lax.axis_size("exp") <= LANES:
+        return fused_layer(
+            attended, out_proj, residual, norm_gain, routes, combine, w_gate, w_up, w_down
+        )
     term = jnp.dot(attended, out_proj, preferred_element_type=jnp.float32)
     mixed = lax.psum_scatter(
         lax.optimization_barrier(term.astype(jnp.bfloat16))
@@ -87,9 +498,11 @@
     capacity = min(tok_count, max(2, tok_count * per_token * 5 // (4 * experts)))
     pair_count = tok_count * per_token
     flat_routes = routes.reshape(pair_count)
-    expert_hot = (flat_routes[:, None] == jnp.arange(experts)[None, :]).astype(jnp.int32)
-    earlier = jnp.cumsum(expert_hot, axis=0) - expert_hot
-    slot_index = jnp.sum(earlier * expert_hot, axis=1)
+    expert_hot = (flat_routes[:, None] == jnp.arange(experts)[None, :]).astype(jnp.float32)
+    pair_ids = jnp.arange(pair_count)
+    before = (pair_ids[:, None] > pair_ids[None, :]).astype(jnp.float32)
+    earlier = jnp.dot(before, expert_hot, preferred_element_type=jnp.float32)
+    slot_index = jnp.sum(earlier * expert_hot, axis=1).astype(jnp.int32)
     position = flat_routes * capacity + slot_index
     position_hot = (position[:, None] == jnp.arange(experts * capacity)[None, :]).astype(
         jnp.float32

time: 317 us -> 171 us (0.54)
  the two profiles are of different devices: /device:TPU:14 before, /device:TPU:0 now
where the time goes in v1:
time: 171 us; the launch traced here: 170 us
  Pallas kernels  158 us (92%)
  local copies, waits for them, and re-layouts  5.52 us (3%)
  matrix products  2.5 us (1%)
  starting transfers between devices  2.4 us (1%)
  other arithmetic  2.02 us (1%)
    pallas_call x1, Pallas kernels, fused_layer(): pl.pallas_call(functools.partial(layer_kernel, sizes), out_shape=jax.Shap...  158 us
  transfers between devices with their start and end apart: 1, of which 0 were waited for; matrix products, arithmetic and copies ran while one was open for 1% of the time, Pallas kernels for 0%

profile of v1, /device:TPU:0, one launch (start us, length us, event | category | flops | bytes accessed | tf_op | source)
XLA Modules:
  0.0 170.3 jit_solution(9965151928821128429)
XLA Ops:
  0.0 0.0 copy-start
  0.0 0.0 copy-start.1
  0.0 0.0 copy-start.3
  0.0 0.0 copy-start.4
  0.0 0.0 copy-start.2
  0.0 1.1 copy.49
  1.2 1.1 copy.38
  2.3 0.1 pad_maximum_fusion
  2.3 2.4 %collective-permute-start = (bf16[2,512,256]{1,2,0:T(8,128)(2,1)S(1)}, bf16[2,512,256]{1,2,0:T(8,128)(2,1)S(1)}, u32[]{:S(2)}, u32[]{:S(2)}) collective-permute-start(bf16[2,512,256]{1,2,0:T(8,128)(2,1)S(1)} %pad_maximum_fusion), channel_id=1, source_target_pairs={{0,16},{1,17},{2,18},{3,19},{4,20},{5,21},{6,22},{7,23},{8,24},{9,... | collective-permute-start | bytes 1572872 | tf_op jit(solution)/shard_map/ppermute | solution.py:422
  4.7 0.0 copy-done.3
  4.7 0.1 copy.44
  4.8 0.0 copy-done.4
  4.8 0.1 copy.45
  4.9 0.0 copy-done.2
  4.9 0.6 reshape.24.gain_ref
  5.5 0.1 iota_compare_fusion
  5.6 0.7 select_reduce_fusion.weigh_ref
  6.3 0.0 copy-done
  6.3 0.0 copy-done.1
  6.3 0.5 fusion.1
  6.9 0.0 collective-permute-done
  7.0 0.5 bitcast_reduce_fusion
  7.5 0.6 fusion.4
  8.1 0.5 fusion.2
  8.6 0.7 fusion.7
  9.4 0.7 fusion.10
  10.1 0.8 copy.50.attended_ref
  10.9 157.8 %shard_map.109 = bf16[32,3584]{1,0:T(8,128)(2,1)} custom-call(bf16[512,256]{1,0:T(8,128)(2,1)} %copy.50.attended_ref, bf16[256,3584]{1,0:T(8,128)(2,1)} %proj_ref.1, bf16[32,3584]{1,0:T(8,128)(2,1)} %residual_ref.1, f32[1,3584]{1,0:T(1,128)} %reshape.24.gain_ref, f32[32,128]{1,0:T(8,128)} %select_reduce_fusion.weigh_ref, bf16[3584,512]{1,0:T(8,128)(2,1)} %bitcast.82, ...), custom_call_target="tpu_custom_call" | custom-call | tf_op jit(solution)/shard_map/pallas_call | solution.py:398
  168.7 1.6 copy.72
  (3 shorter events, 0.1 us)
Async XLA Ops:
  0.0 6.3 %copy-start = (bf16[512,256]{1,0:T(8,128)(2,1)S(1)}, bf16[512,256]{1,0:T(8,128)(2,1)}, u32[]{:S(2)}) copy-start(bf16[512,256]{1,0:T(8,128)(2,1)} %param.11) | copy-start | bytes 786436
  0.0 6.3 %copy-start.1 = (bf16[512,256]{1,0:T(8,128)(2,1)S(1)}, bf16[512,256]{1,0:T(8,128)(2,1)}, u32[]{:S(2)}) copy-start(bf16[512,256]{1,0:T(8,128)(2,1)} %param.12) | copy-start | bytes 786436
  0.0 4.7 %copy-start.3 = (s32[32,8]{0,1:T(8,128)S(1)}, s32[32,8]{0,1:T(8,128)}, u32[]{:S(2)}) copy-start(s32[32,8]{0,1:T(8,128)} %param.17) | copy-start | bytes 3076
  0.0 4.8 %copy-start.4 = (f32[32,8]{0,1:T(8,128)S(1)}, f32[32,8]{0,1:T(8,128)}, u32[]{:S(2)}) copy-start(f32[32,8]{0,1:T(8,128)} %param.18) | copy-start | bytes 3076
  0.0 4.9 %copy-start.2 = (f32[3584]{0:T(1024)S(1)}, f32[3584]{0:T(1024)}, u32[]{:S(2)}) copy-start(f32[3584]{0:T(1024)} %param.16) | copy-start | bytes 43012
  2.3 4.6 %collective-permute-start = (bf16[2,512,256]{1,2,0:T(8,128)(2,1)S(1)}, bf16[2,512,256]{1,2,0:T(8,128)(2,1)S(1)}, u32[]{:S(2)}, u32[]{:S(2)}) collective-permute-start(bf16[2,512,256]{1,2,0:T(8,128)(2,1)S(1)} %pad_maximum_fusion), channel_id=1, source_target_pairs={{0,16},{1,17},{2,18},{3,19},{4,20},{5,21},{6,22},{7,23},{8,24},{9,... | collective-permute-start | bytes 1572872 | tf_op jit(solution)/shard_map/ppermute | solution.py:422

commit v2 on v1

--- a/solution.py
+++ b/solution.py
@@ -10,7 +10,9 @@
 
 HD = 128
 LANES = 128
-CHUNKS = 4
+CHUNKS = 7
+MIX_STEPS = (0, 2, 3, 4, 5, 6, 8, 9)
+SUM_STEPS = (0, 1, 3, 4, 5)
 VMEM_BUDGET = 58 * 1024 * 1024
 
 
@@ -181,7 +183,6 @@
 
     flying = {}
     here = (coords["c"], coords["z"], coords["y"], coords["x"])
-    weights[here] = weigh_ref[...]
     weigh_axes = ("z", "y", "x", "c")
 
     def weigh_step(stage):
@@ -213,63 +214,60 @@
             mix_landing[stage], flying["m", chunk, stage],
         )
 
+    def gather_axes(chunk):
+        first, second = order(chunk)
+        return ("z", second, first, "c")
+
+    def token_start(chunk, stage):
+        axes = gather_axes(chunk)
+        flying["t", chunk, stage] = gather_start(tokens, chunk, stage, axes[:stage], axes[stage])
+
     attended = attended_ref[...]
     squares = jnp.zeros((rows, 1), jnp.float32)
-    for step in range(chunks + 3):
-        if step < chunks:
-            span = pl.ds(step * cols, cols)
-            term[step] = (
+    group_rows = gate.shape[1]
+    lane = lax.broadcasted_iota(jnp.int32, (group_rows, LANES), 1)
+
+    def pick(group, number):
+        held = weights[group].reshape(group_rows, LANES)
+        return jnp.sum(jnp.where(lane == number, held, 0.0), axis=1, keepdims=True)
+
+    def advance(chunk, stage, squares):
+        span = pl.ds(chunk * cols, cols)
+        newest = chunk == chunks - 1
+        if stage == 0:
+            term[chunk] = (
                 jnp.dot(attended, proj_ref[:, span], preferred_element_type=jnp.float32)
                 .astype(jnp.bfloat16)
                 .reshape(term.shape[1:])
             )
-            mix_start(step, 0)
-        for stage in (1, 2):
-            chunk = step - stage
-            if 0 <= chunk < chunks:
-                mix_end(chunk, stage - 1)
-                mix_start(chunk, stage)
-        chunk = step - 3
-        if 0 <= chunk < chunks:
-            span = pl.ds(chunk * cols, cols)
+            mix_start(chunk, 0)
+        elif stage < 3:
+            mix_end(chunk, stage - 1)
+            mix_start(chunk, stage)
+        elif stage == 3:
             value = residual_ref[:, span].astype(jnp.float32) + mix_end(chunk, 2)
             stream[:, span] = value
             squares = squares + jnp.sum(value * value, axis=1, keepdims=True)
-        if step < 4:
-            weigh_step(step)
-    inverse = lax.rsqrt(squares / width + norm_eps)
-
-    def gather_axes(chunk):
-        first, second = order(chunk)
-        return ("z", second, first, "c")
-
-    def token_start(chunk, stage):
-        axes = gather_axes(chunk)
-        flying["t", chunk, stage] = gather_start(tokens, chunk, stage, axes[:stage], axes[stage])
-
-    for chunk in range(chunks):
-        span = pl.ds(chunk * cols, cols)
-        tokens[(chunk,) + here] = (stream[:, span] * inverse * gain_ref[:, span]).astype(
-            jnp.bfloat16
-        )
-        token_start(chunk, 0)
-    loads[0].wait()
-    loads[1].wait()
-    group_rows = gate.shape[1]
-    for step in range(1, chunks + 4):
-        for stage in (1, 2, 3):
-            chunk = step - stage
-            if 0 <= chunk < chunks:
-                for copy in flying["t", chunk, stage - 1]:
-                    copy.wait_recv()
-                token_start(chunk, stage)
-        chunk = step - 4
-        if 0 <= chunk < chunks:
-            for copy in flying["t", chunk, 3]:
+            if newest:
+                inverse = lax.rsqrt(squares / width + norm_eps)
+                own_lane = lax.broadcasted_iota(jnp.int32, (rows, LANES), 1)
+                weights[here] = jnp.where(own_lane == LANES - 1, inverse, weigh_ref[...])
+                weigh_step(0)
+            tokens[(chunk,) + here] = (value * gain_ref[:, span]).astype(jnp.bfloat16)
+            token_start(chunk, 0)
+        else:
+            if newest:
+                weigh_step(stage - 3)
+            for copy in flying["t", chunk, stage - 4]:
                 copy.wait_recv()
-            span = pl.ds(chunk * cols, cols)
-
-            def grow(group, carry, chunk=chunk, span=span):
+            if stage < 7:
+                token_start(chunk, stage - 3)
+                return squares
+            if chunk == 0:
+                loads[0].wait()
+                loads[1].wait()
+
+            def grow(group, carry):
                 piece = tokens[chunk, group].reshape(group_rows, cols)
                 more_gate = jnp.dot(piece, gate_w[span, :], preferred_element_type=jnp.float32)
                 more_upper = jnp.dot(piece, up_w[span, :], preferred_element_type=jnp.float32)
@@ -280,12 +278,19 @@
                     gate[group] = more_gate
                     upper[group] = more_upper
                 else:
-                    act[group] = (jax.nn.silu(more_gate) * more_upper).astype(jnp.bfloat16)
+                    inverse = pick(group, LANES - 1)
+                    act[group] = (
+                        jax.nn.silu(more_gate * inverse) * (more_upper * inverse)
+                    ).astype(jnp.bfloat16)
                 return carry
 
             lax.fori_loop(0, sizes["c"], grow, 0)
-
-    weigh_step(4)
+        return squares
+
+    for step in range(chunks + MIX_STEPS[-1]):
+        for stage, delay in enumerate(MIX_STEPS):
+            if 0 <= step - delay < chunks:
+                squares = advance(step - delay, stage, squares)
     loads[2].wait()
 
     all_axes = ("c", "z", "y", "x")
@@ -308,15 +313,13 @@
             sum_landing[stage], flying["s", chunk, stage],
         )
 
-    lane = lax.broadcasted_iota(jnp.int32, (group_rows, LANES), 1)
-    for step in range(chunks + 4):
+    for step in range(chunks + SUM_STEPS[-1]):
         if step < chunks:
             span = pl.ds(step * cols, cols)
 
             def project(ahead, carry, step=step, span=span):
                 group = lax.rem(coords["c"] + ahead, sizes["c"])
-                held = weights[group].reshape(group_rows, LANES)
-                scale = jnp.sum(jnp.where(lane == where_exp, held, 0.0), axis=1, keepdims=True)
+                scale = pick(group, where_exp)
                 value = jnp.dot(act[group], down_w[:, span], preferred_element_type=jnp.float32)
                 parts[step, group] = (
                     (value * scale).astype(jnp.bfloat16).reshape(parts.shape[2:])
@@ -326,11 +329,11 @@
             lax.fori_loop(0, sizes["c"], project, 0)
             sum_start(step, 0)
         for stage in (1, 2, 3):
-            chunk = step - stage
+            chunk = step - SUM_STEPS[stage]
             if 0 <= chunk < chunks:
                 sum_end(chunk, stage - 1)
                 sum_start(chunk, stage)
-        chunk = step - 4
+        chunk = step - SUM_STEPS[4]
         if 0 <= chunk < chunks:
             span = pl.ds(chunk * cols, cols)
             out_ref[:, span] = (stream[:, span] + sum_end(chunk, 3)).astype(jnp.bfloat16)
@@ -475,7 +478,7 @@
     _, scratch_bytes = layer_scratch(
         layer_sizes(), tok_count, residual.shape[1], w_gate.shape[2]
     )
-    if scratch_bytes < VMEM_BUDGET - 8 * 1024 * 1024 and lax.axis_size("exp") <= LANES:
+    if scratch_bytes < VMEM_BUDGET - 8 * 1024 * 1024 and lax.axis_size("exp") < LANES:
         return fused_layer(
             attended, out_proj, residual, norm_gain, routes, combine, w_gate, w_up, w_down
         )

time: 171 us -> 141 us (0.82)
  Pallas kernels: 158 us -> 128 us
    pallas_call x1, Pallas kernels: 158 us -> 128 us  [fused_layer(): pl.pallas_call(functools.partial(layer_kernel, sizes), out_shape=jax.Shap...]
  transfers between devices with their start and end apart: 1 -> 1, of which waited for: 0 -> 0; matrix products, arithmetic and copies ran while one was open for 1% -> 2% of each run, Pallas kernels for 0% -> 0%
where the time goes in v2:
time: 141 us
  Pallas kernels  128 us (91%)
  local copies, waits for them, and re-layouts  5.52 us (4%)
  matrix products  2.5 us (2%)
  starting transfers between devices  2.4 us (2%)
  other arithmetic  2.02 us (1%)
    pallas_call x1, Pallas kernels, fused_layer(): pl.pallas_call(functools.partial(layer_kernel, sizes), out_shape=jax.Shap...  128 us
    unnamed x14, local copies, waits for them, and re-layouts  2.9 us
  transfers between devices with their start and end apart: 1, of which 0 were waited for; matrix products, arithmetic and copies ran while one was open for 2% of the time, Pallas kernels for 0%

profile of v2, /device:TPU:0, one launch (start us, length us, event | category | flops | bytes accessed | tf_op | source)
XLA Modules:
  0.0 140.8 jit_solution(5987951769009175422)
XLA Ops:
  0.0 0.0 copy-start
  0.0 0.0 copy-start.1
  0.0 0.0 copy-start.3
  0.0 0.0 copy-start.4
  0.0 0.0 copy-start.2
  0.0 1.1 copy.49
  1.2 1.1 copy.38
  2.3 0.1 pad_maximum_fusion
  2.3 2.4 %collective-permute-start = (bf16[2,512,256]{1,2,0:T(8,128)(2,1)S(1)}, bf16[2,512,256]{1,2,0:T(8,128)(2,1)S(1)}, u32[]{:S(2)}, u32[]{:S(2)}) collective-permute-start(bf16[2,512,256]{1,2,0:T(8,128)(2,1)S(1)} %pad_maximum_fusion), channel_id=1, source_target_pairs={{0,16},{1,17},{2,18},{3,19},{4,20},{5,21},{6,22},{7,23},{8,24},{9,... | collective-permute-start | bytes 1572872 | tf_op jit(solution)/shard_map/ppermute | solution.py:425
  4.7 0.0 copy-done.3
  4.7 0.1 copy.44
  4.8 0.0 copy-done.4
  4.8 0.1 copy.45
  4.9 0.0 copy-done.2
  4.9 0.6 reshape.24.gain_ref
  5.5 0.1 iota_compare_fusion
  5.6 0.7 select_reduce_fusion.weigh_ref
  6.3 0.0 copy-done
  6.3 0.0 copy-done.1
  6.3 0.5 fusion.1
  6.9 0.0 collective-permute-done
  7.0 0.5 bitcast_reduce_fusion
  7.5 0.6 fusion.4
  8.1 0.5 fusion.2
  8.6 0.7 fusion.7
  9.4 0.7 fusion.10
  10.1 0.8 copy.50.attended_ref
  10.9 128.2 %shard_map.109 = bf16[32,3584]{1,0:T(8,128)(2,1)} custom-call(bf16[512,256]{1,0:T(8,128)(2,1)} %copy.50.attended_ref, bf16[256,3584]{1,0:T(8,128)(2,1)} %proj_ref.1, bf16[32,3584]{1,0:T(8,128)(2,1)} %residual_ref.1, f32[1,3584]{1,0:T(1,128)} %reshape.24.gain_ref, f32[32,128]{1,0:T(8,128)} %select_reduce_fusion.weigh_ref, bf16[3584,512]{1,0:T(8,128)(2,1)} %bitcast.82, ...), custom_call_target="tpu_custom_call" | custom-call | tf_op jit(solution)/shard_map/pallas_call | solution.py:401
  139.1 1.6 %copy.72 = bf16[32,3584]{1,0:T(8,128)(2,1)} copy(bf16[32,3584]{1,0:T(8,128)(2,1)} %shard_map.109) | data formatting | bytes 458752
  (3 shorter events, 0.1 us)
Async XLA Ops:
  0.0 6.3 %copy-start = (bf16[512,256]{1,0:T(8,128)(2,1)S(1)}, bf16[512,256]{1,0:T(8,128)(2,1)}, u32[]{:S(2)}) copy-start(bf16[512,256]{1,0:T(8,128)(2,1)} %param.11) | copy-start | bytes 786436
  0.0 6.3 %copy-start.1 = (bf16[512,256]{1,0:T(8,128)(2,1)S(1)}, bf16[512,256]{1,0:T(8,128)(2,1)}, u32[]{:S(2)}) copy-start(bf16[512,256]{1,0:T(8,128)(2,1)} %param.12) | copy-start | bytes 786436
  0.0 4.7 %copy-start.3 = (s32[32,8]{0,1:T(8,128)S(1)}, s32[32,8]{0,1:T(8,128)}, u32[]{:S(2)}) copy-start(s32[32,8]{0,1:T(8,128)} %param.17) | copy-start | bytes 3076
  0.0 4.8 %copy-start.4 = (f32[32,8]{0,1:T(8,128)S(1)}, f32[32,8]{0,1:T(8,128)}, u32[]{:S(2)}) copy-start(f32[32,8]{0,1:T(8,128)} %param.18) | copy-start | bytes 3076
  0.0 4.9 %copy-start.2 = (f32[3584]{0:T(1024)S(1)}, f32[3584]{0:T(1024)}, u32[]{:S(2)}) copy-start(f32[3584]{0:T(1024)} %param.16) | copy-start | bytes 43012
  2.3 4.6 %collective-permute-start = (bf16[2,512,256]{1,2,0:T(8,128)(2,1)S(1)}, bf16[2,512,256]{1,2,0:T(8,128)(2,1)S(1)}, u32[]{:S(2)}, u32[]{:S(2)}) collective-permute-start(bf16[2,512,256]{1,2,0:T(8,128)(2,1)S(1)} %pad_maximum_fusion), channel_id=1, source_target_pairs={{0,16},{1,17},{2,18},{3,19},{4,20},{5,21},{6,22},{7,23},{8,24},{9,... | collective-permute-start | bytes 1572872 | tf_op jit(solution)/shard_map/ppermute | solution.py:425
